TPU v7x, 32 devices: a whole 2x2x4 slice. The times are simulated.
32 devices in a mesh: dp: 16 (over z, x, core), tensor: 2 (over y).
Axes of the slice: x: 2, y: 2, z: 4, core: 2. Of those that a mesh axis runs over, the one named last changes fastest.
Arguments:
- inputs: bfloat16 [4096, 1024], P(('dp', 'tensor')), may hold values from -6 to 6
- segment_ids: int32 [4096], P('dp'), may hold values from 0 to 4, as said below
- gain_in: float32 [1024], replicated, may hold values from 0.1 to 1.9
- w_query: bfloat16 [1024, 1024], P('dp', 'tensor'), may hold values from -0.1875 to 0.1875
- w_key: bfloat16 [1024, 1024], P('dp', 'tensor'), may hold values from -0.1875 to 0.1875
- w_value: bfloat16 [1024, 2048], P('dp', 'tensor'), may hold values from -0.1875 to 0.1875
- w_gate: bfloat16 [1024, 2048], P('dp', 'tensor'), may hold values from -0.1875 to 0.1875
- w_decay: bfloat16 [1024, 2, 8], P('dp', None, 'tensor'), may hold values from -0.1875 to 0.1875
- conv_query: float32 [4, 1024], replicated, may hold values from -3 to 3
- conv_key: float32 [4, 1024], replicated, may hold values from -3 to 3
- conv_value: float32 [4, 2048], replicated, may hold values from -3 to 3
- a_log: float32 [8], replicated, may hold values from 0 to 2.77
- dt_bias: float32 [8], replicated, may hold values from -6.9 to -2.3
- gain_mix: float32 [256], replicated, may hold values from 0.1 to 1.9
- w_out: bfloat16 [2048, 1024], P('tensor', 'dp'), may hold values from -0.125 to 0.125
- gain_ffn: float32 [1024], replicated, may hold values from 0.1 to 1.9
- w_ffn_gate: bfloat16 [1024, 2816], P('dp', 'tensor'), may hold values from -0.1875 to 0.1875
- w_ffn_up: bfloat16 [1024, 2816], P('dp', 'tensor'), may hold values from -0.1875 to 0.1875
- w_ffn_down: bfloat16 [2816, 1024], P('tensor', 'dp'), may hold values from -0.15625 to 0.15625
- out_grad: bfloat16 [4096, 1024], P(('dp', 'tensor')), may hold values from -6 to 6
Outputs:
- output: bfloat16 [4096, 1024], P(('dp', 'tensor'))
- grad_inputs: float32 [4096, 1024], P(('dp', 'tensor'))
- grad_gain_in: float32 [1024], replicated
- grad_w_query: float32 [1024, 1024], P('dp', 'tensor')
- grad_w_key: float32 [1024, 1024], P('dp', 'tensor')
- grad_w_value: float32 [1024, 2048], P('dp', 'tensor')
- grad_w_gate: float32 [1024, 2048], P('dp', 'tensor')
- grad_w_decay: float32 [1024, 2, 8], P('dp', None, 'tensor')
- grad_conv_query: float32 [4, 1024], replicated
- grad_conv_key: float32 [4, 1024], replicated
- grad_conv_value: float32 [4, 2048], replicated
- grad_a_log: float32 [8], replicated
- grad_dt_bias: float32 [8], replicated
- mixer_gain_gradient: float32 [256], replicated
- grad_w_out: float32 [2048, 1024], P('tensor', 'dp')
- grad_gain_ffn: float32 [1024], replicated
- grad_w_ffn_gate: float32 [1024, 2816], P('dp', 'tensor')
- grad_w_ffn_up: float32 [1024, 2816], P('dp', 'tensor')
- grad_w_ffn_down: float32 [2816, 1024], P('tensor', 'dp')
Inputs may be any that keep to these rules, and one draw needn't show every extreme that they name: `segment_ids`: in each aligned block of 256 tokens the ids start at 0 and rise by one at each new segment, never falling; every block holds exactly 5 segments, and one of them covers tokens 256 // 4 to 192 of the block.
All inputs are finite; a program needn't handle non-finite values.
Results may differ from a plain program's by a relative error of at most 0.0131.
Values may be sent and summed in bfloat16 or wider, within the bound.
A program may use at most 192 MiB of HBM per device.

v0:
```python
import jax
import jax.numpy as jnp
from jax import lax
from jax.sharding import PartitionSpec as P

SPAN = 64


highest = lax.Precision.HIGHEST
norm_epsilon = 1e-06


def rms_rows(matrix):
    return matrix * lax.rsqrt(jnp.mean(matrix * matrix, axis=-1, keepdims=True) + norm_epsilon)


def rms_back(matrix, incoming, gain):
    scale = lax.rsqrt(jnp.mean(matrix * matrix, axis=-1, keepdims=True) + norm_epsilon)
    normed = matrix * scale
    scaled = incoming * gain
    grad_matrix = scale * (scaled - normed * jnp.mean(scaled * normed, axis=-1, keepdims=True))
    return (grad_matrix, jnp.sum(incoming * normed, axis=0))


def contract_last(left, right):
    return lax.dot_general(
        left, right, (((1,), (1,)), ((), ())), preferred_element_type=jnp.float32
    )


def contract_first(left, right):
    return lax.dot_general(
        left, right, (((0,), (0,)), ((), ())), preferred_element_type=jnp.float32
    )


def causal_conv(input_signal, kernel, segment_ids):
    length = input_signal.shape[0]
    widths = kernel.shape[0]
    summed = input_signal * kernel[widths - 1]
    for offset in range(1, widths):
        shifted = jnp.concatenate(
            [
                jnp.zeros((offset, input_signal.shape[1]), jnp.float32),
                input_signal[: length - offset],
            ],
            axis=0,
        )
        shifted_ids = jnp.concatenate(
            [jnp.full((offset,), -1, jnp.int32), segment_ids[: length - offset]]
        )
        matches = (shifted_ids == segment_ids).astype(jnp.float32)
        summed = summed + shifted * kernel[widths - 1 - offset] * matches[:, None]
    return jax.nn.silu(summed)


def unit_heads(tensor3, factor):
    return (
        tensor3
        * lax.rsqrt(jnp.sum(tensor3 * tensor3, axis=-1, keepdims=True) + norm_epsilon)
        * factor
    )


def segment_update(state_holder, segment_parts):
    running_state, closing_segment = state_holder
    span_query, span_keys, span_values, span_strength, span_decay, span_ids = segment_parts
    block_len = span_ids.shape[0]
    cumulative = jnp.cumsum(span_decay, axis=-1)
    row_index = lax.broadcasted_iota(jnp.int32, (block_len, block_len), 0)
    col_index = lax.broadcasted_iota(jnp.int32, (block_len, block_len), 1)
    same_seg = span_ids[:, None] == span_ids[None, :]
    lower_mask = jnp.logical_and(row_index >= col_index, same_seg).astype(jnp.float32)
    strict = jnp.logical_and(row_index > col_index, same_seg).astype(jnp.float32)
    difference = cumulative[:, :, None] - cumulative[:, None, :]
    within = jnp.exp(jnp.minimum(difference, 0.0))
    carried = (span_ids == closing_segment).astype(jnp.float32)
    entering = jnp.exp(cumulative) * carried[None, :]
    inner_kk = jnp.einsum("hid,hjd->hij", span_keys, span_keys, precision=highest)
    system = (
        jnp.eye(block_len, dtype=jnp.float32)[None]
        + span_strength[:, :, None] * inner_kk * within * strict[None]
    )
    from_state = jnp.einsum("hid,hde->hie", span_keys, running_state, precision=highest)
    target = span_strength[:, :, None] * (span_values - entering[:, :, None] * from_state)
    solved = lax.linalg.triangular_solve(
        system,
        target,
        left_side=True,
        lower=True,
        transpose_a=False,
        conjugate_a=False,
        unit_diagonal=True,
    )
    inner_qk = jnp.einsum("hid,hjd->hij", span_query, span_keys, precision=highest)
    result = entering[:, :, None] * jnp.einsum(
        "hid,hde->hie", span_query, running_state, precision=highest
    )
    result = result + jnp.einsum(
        "hij,hje->hie", inner_qk * within * lower_mask[None], solved, precision=highest
    )
    tail_weight = within[:, block_len - 1, :] * lower_mask[block_len - 1][None, :]
    new_state = entering[:, block_len - 1][:, None, None] * running_state
    new_state = new_state + jnp.einsum(
        "hjd,hje->hde", span_keys * tail_weight[:, :, None], solved, precision=highest
    )
    return ((new_state, span_ids[block_len - 1]), result)


def delta_rule(query_heads, key_heads, value_heads, strength, decay_log, segment_ids):
    head_count, length = strength.shape
    blocks_count = length // SPAN

    def cut_blocks(tensor):
        return jnp.moveaxis(
            tensor.reshape((head_count, blocks_count, SPAN) + tensor.shape[2:]), 1, 0
        )

    segment_parts = (
        cut_blocks(query_heads),
        cut_blocks(key_heads),
        cut_blocks(value_heads),
        cut_blocks(strength),
        cut_blocks(decay_log),
        segment_ids.reshape(blocks_count, SPAN),
    )
    initial = (
        jnp.zeros((head_count, query_heads.shape[2], value_heads.shape[2]), jnp.float32),
        jnp.int32(-1),
    )
    final_state, results = lax.scan(jax.checkpoint(segment_update), initial, segment_parts)
    return jnp.moveaxis(results, 0, 1).reshape(head_count, length, value_heads.shape[2])


def mixing_core(
    query_raw,
    key_raw,
    value_raw,
    gate_raw,
    decay_raw,
    segment_ids,
    conv_query,
    conv_key,
    conv_value,
    a_log,
    dt_bias,
    gain_mix,
):
    length = query_raw.shape[0]
    head_count = a_log.shape[0]
    head_dim = query_raw.shape[1] // head_count
    value_dim = gain_mix.shape[0]
    query_heads = unit_heads(
        causal_conv(query_raw, conv_query, segment_ids).reshape(length, head_count, head_dim),
        head_dim ** (-0.5),
    )
    key_heads = unit_heads(
        causal_conv(key_raw, conv_key, segment_ids).reshape(length, head_count, head_dim), 1.0
    )
    value_heads = causal_conv(value_raw, conv_value, segment_ids).reshape(
        length, head_count, value_dim
    )
    strength = jax.nn.sigmoid(decay_raw[:, 1, :])
    decay_log = -jnp.exp(a_log) * jax.nn.softplus(decay_raw[:, 0, :] + dt_bias)
    mixed_heads = delta_rule(
        jnp.transpose(query_heads, (1, 0, 2)),
        jnp.transpose(key_heads, (1, 0, 2)),
        jnp.transpose(value_heads, (1, 0, 2)),
        strength.T,
        decay_log.T,
        segment_ids,
    )
    mixed_heads = jnp.transpose(mixed_heads, (1, 0, 2))
    normed = (
        mixed_heads
        * lax.rsqrt(jnp.mean(mixed_heads * mixed_heads, axis=-1, keepdims=True) + norm_epsilon)
        * gain_mix
    )
    gated = normed * jax.nn.silu(gate_raw.reshape(length, head_count, value_dim))
    return gated.reshape(length, head_count * value_dim)


def sum_ffn_grads(grad_fgate_w, grad_fup_w, grad_fdown_t):
    summed = (
        lax.psum_scatter(grad_fgate_w, "dp", scatter_dimension=0, tiled=True),
        lax.psum_scatter(grad_fup_w, "dp", scatter_dimension=0, tiled=True),
        lax.psum_scatter(grad_fdown_t, "dp", scatter_dimension=0, tiled=True),
    )
    return (summed[0], summed[1], summed[2].T)


def per_device(
    inputs,
    segment_ids,
    gain_in,
    w_query,
    w_key,
    w_value,
    w_gate,
    w_decay,
    conv_query,
    conv_key,
    conv_value,
    a_log,
    dt_bias,
    gain_mix,
    w_out,
    gain_ffn,
    w_ffn_gate,
    w_ffn_up,
    w_ffn_down,
    out_grad,
):
    rank_tensor = lax.axis_index("tensor")
    head_count = w_decay.shape[2]
    key_width = w_query.shape[1]
    value_width = w_value.shape[1]
    conv_q_part = lax.dynamic_slice_in_dim(conv_query, rank_tensor * key_width, key_width, 1)
    conv_k_part = lax.dynamic_slice_in_dim(conv_key, rank_tensor * key_width, key_width, 1)
    conv_v_part = lax.dynamic_slice_in_dim(conv_value, rank_tensor * value_width, value_width, 1)
    a_log_part = lax.dynamic_slice_in_dim(a_log, rank_tensor * head_count, head_count, 0)
    dt_bias_part = lax.dynamic_slice_in_dim(dt_bias, rank_tensor * head_count, head_count, 0)
    inputs_wide = inputs.astype(jnp.float32)
    normed_in = lax.all_gather(
        (rms_rows(inputs_wide) * gain_in).astype(jnp.bfloat16), "tensor", axis=0, tiled=True
    )
    full_query, full_key, full_value, full_gate, full_decay, full_out = (
        lax.all_gather(w_query, "dp", axis=0, tiled=True),
        lax.all_gather(w_key, "dp", axis=0, tiled=True),
        lax.all_gather(w_value, "dp", axis=0, tiled=True),
        lax.all_gather(w_gate, "dp", axis=0, tiled=True),
        lax.all_gather(w_decay, "dp", axis=0, tiled=True),
        lax.all_gather(w_out, "dp", axis=1, tiled=True),
    )
    model_width = full_query.shape[0]
    decay_flat = full_decay.reshape(model_width, 2 * head_count)
    query_raw = jnp.dot(normed_in, full_query, preferred_element_type=jnp.float32)
    key_raw = jnp.dot(normed_in, full_key, preferred_element_type=jnp.float32)
    value_raw = jnp.dot(normed_in, full_value, preferred_element_type=jnp.float32)
    gate_raw = jnp.dot(normed_in, full_gate, preferred_element_type=jnp.float32)
    decay_raw = jnp.dot(normed_in, decay_flat, preferred_element_type=jnp.float32).reshape(
        -1, 2, head_count
    )

    def core_local(
        query_in,
        key_in,
        value_in,
        gate_in,
        decay_in,
        conv_q_in,
        conv_k_in,
        conv_v_in,
        a_log_in,
        dt_bias_in,
        gain_mix_in,
    ):
        return mixing_core(
            query_in,
            key_in,
            value_in,
            gate_in,
            decay_in,
            segment_ids,
            conv_q_in,
            conv_k_in,
            conv_v_in,
            a_log_in,
            dt_bias_in,
            gain_mix_in,
        )

    mixed_out, core_back = jax.vjp(
        core_local,
        query_raw,
        key_raw,
        value_raw,
        gate_raw,
        decay_raw,
        conv_q_part,
        conv_k_part,
        conv_v_part,
        a_log_part,
        dt_bias_part,
        gain_mix,
    )
    mixed_gated = mixed_out.astype(jnp.bfloat16)
    mixer_terms = jnp.dot(mixed_gated, full_out, preferred_element_type=jnp.float32)
    residual = inputs_wide + lax.psum_scatter(
        mixer_terms, "tensor", scatter_dimension=0, tiled=True
    )
    normed_mid = lax.all_gather(
        (rms_rows(residual) * gain_ffn).astype(jnp.bfloat16), "tensor", axis=0, tiled=True
    )
    full_fgate, full_fup, full_fdown = (
        lax.all_gather(w_ffn_gate, "dp", axis=0, tiled=True),
        lax.all_gather(w_ffn_up, "dp", axis=0, tiled=True),
        lax.all_gather(w_ffn_down, "dp", axis=1, tiled=True),
    )
    ffn_gate = jnp.dot(normed_mid, full_fgate, preferred_element_type=jnp.float32)
    ffn_up = jnp.dot(normed_mid, full_fup, preferred_element_type=jnp.float32)
    hidden = (jax.nn.silu(ffn_gate) * ffn_up).astype(jnp.bfloat16)
    ffn_terms = jnp.dot(hidden, full_fdown, preferred_element_type=jnp.float32)
    output = (
        residual
        + lax.psum_scatter(
            ffn_terms.astype(jnp.bfloat16), "tensor", scatter_dimension=0, tiled=True
        ).astype(jnp.float32)
    ).astype(jnp.bfloat16)
    grad_rows_out = lax.all_gather(out_grad, "tensor", axis=0, tiled=True)
    back_fgate, back_fup, back_fdown = (full_fgate, full_fup, full_fdown)
    grad_hidden = contract_last(grad_rows_out, back_fdown)
    grad_fdown_turned = contract_first(grad_rows_out, hidden)
    sigmoid_gate = jax.nn.sigmoid(ffn_gate)
    grad_fgate = (
        grad_hidden * ffn_up * sigmoid_gate * (1.0 + ffn_gate * (1.0 - sigmoid_gate))
    ).astype(jnp.bfloat16)
    grad_fup = (grad_hidden * (ffn_gate * sigmoid_gate)).astype(jnp.bfloat16)
    grad_w_ffn_gate = contract_first(normed_mid, grad_fgate)
    grad_w_ffn_up = contract_first(normed_mid, grad_fup)
    mid_terms = contract_last(grad_fgate, back_fgate) + contract_last(grad_fup, back_fup)
    grad_mid = lax.psum_scatter(
        mid_terms.astype(jnp.bfloat16), "tensor", scatter_dimension=0, tiled=True
    ).astype(jnp.float32)
    grad_mid_rows, grad_gain_ffn = rms_back(residual, grad_mid, gain_ffn)
    grad_resid = out_grad.astype(jnp.float32) + grad_mid_rows
    grad_rows_mid = lax.all_gather(grad_resid.astype(jnp.bfloat16), "tensor", axis=0, tiled=True)
    grad_mixed = contract_last(grad_rows_mid, full_out)
    grad_out_turned = contract_first(grad_rows_mid, mixed_gated)
    (
        grad_query,
        grad_key,
        grad_value,
        grad_gate,
        grad_decay,
        grad_conv_q,
        grad_conv_k,
        grad_conv_v,
        grad_a_part,
        grad_dt_part,
        mixer_gain_gradient,
    ) = core_back(grad_mixed)
    query_low = grad_query.astype(jnp.bfloat16)
    key_low = grad_key.astype(jnp.bfloat16)
    value_low = grad_value.astype(jnp.bfloat16)
    gate_low = grad_gate.astype(jnp.bfloat16)
    decay_low = grad_decay.reshape(-1, 2 * head_count).astype(jnp.bfloat16)
    in_terms = (
        contract_last(query_low, full_query)
        + contract_last(key_low, full_key)
        + contract_last(value_low, full_value)
    )
    in_terms = in_terms + contract_last(gate_low, full_gate) + contract_last(decay_low, decay_flat)
    grad_w_query = contract_first(normed_in, query_low)
    grad_w_key = contract_first(normed_in, key_low)
    grad_w_value = contract_first(normed_in, value_low)
    grad_w_gate = contract_first(normed_in, gate_low)
    grad_w_decay = contract_first(normed_in, decay_low).reshape(model_width, 2, head_count)
    grad_in = lax.psum_scatter(
        in_terms.astype(jnp.bfloat16), "tensor", scatter_dimension=0, tiled=True
    ).astype(jnp.float32)
    grad_in_rows, grad_gain_in = rms_back(inputs_wide, grad_in, gain_in)
    grad_inputs = grad_resid + grad_in_rows
    ffn_shards = sum_ffn_grads(grad_w_ffn_gate, grad_w_ffn_up, grad_fdown_turned)
    mixer_shards = (
        lax.psum_scatter(grad_w_query, "dp", scatter_dimension=0, tiled=True),
        lax.psum_scatter(grad_w_key, "dp", scatter_dimension=0, tiled=True),
        lax.psum_scatter(grad_w_value, "dp", scatter_dimension=0, tiled=True),
        lax.psum_scatter(grad_w_gate, "dp", scatter_dimension=0, tiled=True),
        lax.psum_scatter(grad_w_decay, "dp", scatter_dimension=0, tiled=True),
        lax.psum_scatter(grad_out_turned, "dp", scatter_dimension=0, tiled=True),
    )

    def place_part(part_grad, whole, along):
        return lax.dynamic_update_slice_in_dim(
            jnp.zeros(whole.shape, jnp.float32),
            part_grad,
            rank_tensor * part_grad.shape[along],
            along,
        )

    small = lax.psum(
        (
            grad_gain_in,
            place_part(grad_conv_q, conv_query, 1),
            place_part(grad_conv_k, conv_key, 1),
            place_part(grad_conv_v, conv_value, 1),
            place_part(grad_a_part, a_log, 0),
            place_part(grad_dt_part, dt_bias, 0),
            mixer_gain_gradient,
            grad_gain_ffn,
        ),
        ("dp", "tensor"),
    )
    return (
        output,
        grad_inputs,
        small[0],
        mixer_shards[0],
        mixer_shards[1],
        mixer_shards[2],
        mixer_shards[3],
        mixer_shards[4],
        small[1],
        small[2],
        small[3],
        small[4],
        small[5],
        small[6],
        mixer_shards[5].T,
        small[7],
        ffn_shards[0],
        ffn_shards[1],
        ffn_shards[2],
    )


def solution(mesh):
    placed = (
        P(("dp", "tensor"), None),
        P("dp"),
        P(),
        P("dp", "tensor"),
        P("dp", "tensor"),
        P("dp", "tensor"),
        P("dp", "tensor"),
        P("dp", None, "tensor"),
        P(),
        P(),
        P(),
        P(),
        P(),
        P(),
        P("tensor", "dp"),
        P(),
        P("dp", "tensor"),
        P("dp", "tensor"),
        P("tensor", "dp"),
        P(("dp", "tensor"), None),
    )
    return jax.shard_map(
        per_device,
        mesh=mesh,
        in_specs=placed,
        out_specs=(
            P(("dp", "tensor"), None),
            P(("dp", "tensor"), None),
            P(),
            P("dp", "tensor"),
            P("dp", "tensor"),
            P("dp", "tensor"),
            P("dp", "tensor"),
            P("dp", None, "tensor"),
            P(),
            P(),
            P(),
            P(),
            P(),
            P(),
            P("tensor", "dp"),
            P(),
            P("dp", "tensor"),
            P("dp", "tensor"),
            P("tensor", "dp"),
        ),
        check_vma=False,
    )
```

profile of v0, /device:TPU:0, one launch (start us, length us, event | category | flops | bytes accessed | tf_op | source)
XLA Modules:
  0.0 1611.6 jit_solution(16988430585807510979)
XLA Ops:
  23.1 23.8 %all_gather.40 = bf16[1024,2,4]{2,1,0:T(2,128)(2,1)S(1)} all-gather(bf16[64,2,4]{2,1,0:T(2,128)(2,1)S(1)} %copy.323), channel_id=1, replica_groups=mesh['dp'=16,'tensor'=2] {'dp'}, dimensions={0}, use_global_device_ids=true | all-gather | bytes 17408 | tf_op jit(solution)/shard_map/all_gather | solution.py:232
  53.1 37.7 %all-gather.9.cloned.1.call-done = bf16[1024,512]{1,0:T(8,128)(2,1)} async-done(((bf16[64,512]{1,0:T(8,128)(2,1)}), bf16[1024,512]{1,0:T(8,128)(2,1)}) %all-gather.9.cloned.1.call-update) | async-done | bytes 1048592 | tf_op jit(solution)/shard_map/all_gather | solution.py:229
  99.2 34.1 %all-gather.11.cloned.1.call-done = bf16[1024,1024]{1,0:T(8,128)(2,1)} async-done(((bf16[64,1024]{1,0:T(8,128)(2,1)}), bf16[1024,1024]{1,0:T(8,128)(2,1)}) %all-gather.11.cloned.1.call-update) | async-done | bytes 2097168 | tf_op jit(solution)/shard_map/all_gather | solution.py:230
  138.8 127.9 %while.44 = (s32[]{:T(128)}, f32[4,128,256]{2,1,0:T(8,128)S(1)}, s32[]{:T(128)}, f32[4,4,64,256]{3,2,0,1:T(8,128)S(1)}, f32[4,4,128,256]{3,2,1,0:T(8,128)}, /*in...) while((s32[]{:T(128)}, f32[4,128,256]{2,1,0:T(8,128)S(1)}, ...), condition=%wide.region_5.7_spmd.clone, body=%wide.region_3.6_spmd.clone.sunk | while | flops 454427072 | bytes 6928122 | solution.py:131
  141.2 20.4 %custom-call.24 = f32[4,1,64,64]{2,3,1,0:T(8,128)S(1)} custom-call(f32[4,1,64,64]{3,2,1,0:T(8,128)} %fusion.409), custom_call_target="InvertDiagBlocksLowerTriangular" | custom-call | tf_op jit(solution)/shard_map/jvp()/while/body/eval_jaxpr/triangular_solve/custom-call.1 | solution.py:86
  173.2 20.4 %custom-call.24 = f32[4,1,64,64]{2,3,1,0:T(8,128)S(1)} custom-call(f32[4,1,64,64]{3,2,1,0:T(8,128)} %fusion.409), custom_call_target="InvertDiagBlocksLowerTriangular" | custom-call | tf_op jit(solution)/shard_map/jvp()/while/body/eval_jaxpr/triangular_solve/custom-call.1 | solution.py:86
  312.3 34.2 %all-gather.19.cloned.1.call-done = bf16[1024,1408]{1,0:T(8,128)(2,1)} async-done(((bf16[64,1408]{1,0:T(8,128)(2,1)}), bf16[1024,1408]{1,0:T(8,128)(2,1)}) %all-gather.19.cloned.1.call-update) | async-done | bytes 2883600 | tf_op jit(solution)/shard_map/all_gather | solution.py:296
  350.4 41.4 %all-gather.21.cloned.1.call-done = bf16[1024,1408]{1,0:T(8,128)(2,1)} async-done(((bf16[64,1408]{1,0:T(8,128)(2,1)}), bf16[1024,1408]{1,0:T(8,128)(2,1)}) %all-gather.21.cloned.1.call-update) | async-done | bytes 2883600 | tf_op jit(solution)/shard_map/all_gather | solution.py:297
  395.7 41.4 %all-gather.23.cloned.1.call-done = bf16[1408,1024]{0,1:T(8,128)(2,1)} async-done(((bf16[1408,64]{0,1:T(8,128)(2,1)}), bf16[1408,1024]{0,1:T(8,128)(2,1)}) %all-gather.23.cloned.1.call-update) | async-done | bytes 2883600 | tf_op jit(solution)/shard_map/all_gather | solution.py:298
  479.8 244.7 %while.45 = (s32[]{:T(128)}, f32[4,128,256]{2,1,0:T(8,128)}, f32[4,4,64,128]{3,2,0,1:T(8,128)}, f32[4,4,64,128]{3,2,0,1:T(8,128)}, f32[4,4,64,256]{3,2,0,1:T(8,1...) while((s32[]{:T(128)}, f32[4,128,256]{2,1,0:T(8,128)}, ...), condition=%wide.region_24.26_spmd.clone, body=%wide.region_13.25_spmd.clone.sunk | while | flops 1224000256 | bytes 23688636 | solution.py:131
  489.4 20.4 %custom-call.25 = f32[4,1,64,64]{2,3,1,0:T(8,128)S(1)} custom-call(f32[4,1,64,64]{3,2,1,0:T(8,128)} %get-tuple-element.1256), custom_call_target="InvertDiagBlocksLowerTriangular" | custom-call | tf_op jit(solution)/shard_map/transpose(jvp())/while/body/eval_jaxpr/checkpoint/triangular_solve | solution.py:86
  550.7 20.4 %custom-call.25 = f32[4,1,64,64]{2,3,1,0:T(8,128)S(1)} custom-call(f32[4,1,64,64]{3,2,1,0:T(8,128)} %get-tuple-element.1256), custom_call_target="InvertDiagBlocksLowerTriangular" | custom-call | tf_op jit(solution)/shard_map/transpose(jvp())/while/body/eval_jaxpr/checkpoint/triangular_solve | solution.py:86
  612.1 20.4 %custom-call.25 = f32[4,1,64,64]{2,3,1,0:T(8,128)S(1)} custom-call(f32[4,1,64,64]{3,2,1,0:T(8,128)} %get-tuple-element.1256), custom_call_target="InvertDiagBlocksLowerTriangular" | custom-call | tf_op jit(solution)/shard_map/transpose(jvp())/while/body/eval_jaxpr/checkpoint/triangular_solve | solution.py:86
  673.4 20.4 %custom-call.25 = f32[4,1,64,64]{2,3,1,0:T(8,128)S(1)} custom-call(f32[4,1,64,64]{3,2,1,0:T(8,128)} %get-tuple-element.1256), custom_call_target="InvertDiagBlocksLowerTriangular" | custom-call | tf_op jit(solution)/shard_map/transpose(jvp())/while/body/eval_jaxpr/checkpoint/triangular_solve | solution.py:86
  805.7 24.2 %reduce-scatter.40.cloned.1.call-done = f32[64,8]{1,0:T(8,128)} async-done(((f32[1024,8]{1,0:T(8,128)}), f32[64,8]{1,0:T(8,128)}) %reduce-scatter.40.cloned.1.call-update) | async-done | bytes 2064
  847.9 128.6 %all-reduce.39.cloned.1.call-done = (f32[1024]{0:T(1024)}, f32[4,1024]{1,0:T(4,128)}, f32[4,1024]{1,0:T(4,128)}, f32[4,2048]{1,0:T(4,128)}, f32[8]{0:T(128)}, /*index=5*/f32[8]{0:T(128)}, f32[256]{0:T(256)}, f32[1024]{0:T(1024)}) async-done(((f32[1024]{0:T(1024)}, f32[4,1024]{1,0:T(4,128)}, f32[4,1024]{1,0:T(4,128)}, f32[4,2048]{1,0:T(4,128)}, f32[8]{0:T(128)}, /*index=5*/f32[8]{0:T(128)}, f32[256]{0:T(256)}, ...) | async-done | bytes 74832 | tf_op jit(solution)/shard_map/psum | solution.py:382
  976.5 67.8 %reduce-scatter.28.cloned.1.call-done = f32[64,512]{1,0:T(8,128)} async-done(((f32[1024,512]{1,0:T(8,128)}), f32[64,512]{1,0:T(8,128)}) %reduce-scatter.28.cloned.1.call-update) | async-done | bytes 131088 | tf_op jit(solution)/shard_map/reduce_scatter | solution.py:367
  1044.3 65.2 %reduce-scatter.26.cloned.1.call-done = f32[64,512]{1,0:T(8,128)} async-done(((f32[1024,512]{1,0:T(8,128)}), f32[64,512]{1,0:T(8,128)}) %reduce-scatter.26.cloned.1.call-update) | async-done | bytes 131088 | tf_op jit(solution)/shard_map/reduce_scatter | solution.py:366
  1109.5 75.7 %reduce-scatter.34.cloned.1.call-done = f32[64,1024]{1,0:T(8,128)} async-done(((f32[1024,1024]{1,0:T(8,128)}), f32[64,1024]{1,0:T(8,128)}) %reduce-scatter.34.cloned.1.call-update) | async-done | bytes 262160 | tf_op jit(solution)/shard_map/reduce_scatter | solution.py:371
  1185.2 76.4 %reduce-scatter.30.cloned.1.call-done = f32[64,1024]{1,0:T(8,128)} async-done(((f32[1024,1024]{1,0:T(8,128)}), f32[64,1024]{1,0:T(8,128)}) %reduce-scatter.30.cloned.1.call-update) | async-done | bytes 262160 | tf_op jit(solution)/shard_map/reduce_scatter | solution.py:368
  1261.6 75.8 %reduce-scatter.32.cloned.1.call-done = f32[64,1024]{1,0:T(8,128)} async-done(((f32[1024,1024]{1,0:T(8,128)}), f32[64,1024]{1,0:T(8,128)}) %reduce-scatter.32.cloned.1.call-update) | async-done | bytes 262160 | tf_op jit(solution)/shard_map/reduce_scatter | solution.py:369
  1337.4 85.5 %reduce-scatter.36.cloned.1.call-done = f32[64,1408]{1,0:T(8,128)} async-done(((f32[1024,1408]{1,0:T(8,128)}), f32[64,1408]{1,0:T(8,128)}) %reduce-scatter.36.cloned.1.call-update) | async-done | bytes 360464 | tf_op jit(solution)/shard_map/reduce_scatter | solution.py:185
  1422.9 85.7 %reduce-scatter.38.cloned.1.call-done = f32[64,1408]{1,0:T(8,128)} async-done(((f32[1024,1408]{1,0:T(8,128)}), f32[64,1408]{1,0:T(8,128)}) %reduce-scatter.38.cloned.1.call-update) | async-done | bytes 360464 | tf_op jit(solution)/shard_map/reduce_scatter | solution.py:186
  1508.6 85.8 %reduce-scatter.42.cloned.1.call-done = f32[64,1408]{1,0:T(8,128)} async-done(((f32[1024,1408]{1,0:T(8,128)}), f32[64,1408]{1,0:T(8,128)}) %reduce-scatter.42.cloned.1.call-update) | async-done | bytes 360464
  (929 shorter events, 484.4 us)
Async XLA Ops:
  7.3 44.1 %all-gather.13.cloned.1.call-start = ((), (), s32[]{:S(2)}) async-start(), calls=%async_computation.15 | async-start | bytes 1114112 | tf_op jit(solution)/shard_map/all_gather | solution.py:228
  8.0 82.8 %all-gather.9.cloned.1.call-start = ((), (), s32[]{:S(2)}) async-start(), calls=%async_computation.13 | async-start | bytes 1114112 | tf_op jit(solution)/shard_map/all_gather | solution.py:229
  8.7 124.6 %all-gather.11.cloned.1.call-start = ((), (), s32[]{:S(2)}) async-start(), calls=%async_computation.14 | async-start | bytes 2228224 | tf_op jit(solution)/shard_map/all_gather | solution.py:230
  9.5 257.5 %all-gather.15.cloned.1.call-start = ((), (), s32[]{:S(2)}) async-start(), calls=%async_computation.16 | async-start | bytes 2228224 | tf_op jit(solution)/shard_map/all_gather | solution.py:231
  10.1 262.8 %all-gather.17.cloned.1.call-start = ((), (), s32[]{:S(2)}) async-start(), calls=%async_computation.17 | async-start | bytes 2228224 | tf_op jit(solution)/shard_map/all_gather | solution.py:233
  10.6 290.5 %reduce-scatter.18.cloned.1.call-start = ((), (), s32[]{:S(2)}) async-start(), calls=%async_computation.18 | async-start | bytes 1572864 | tf_op jit(solution)/shard_map/reduce_scatter | solution.py:289
  48.2 87.5 %copy-start.87 = (f32[1,1024]{1,0:T(1,128)}, f32[1,1024]{1,0:T(1,128)S(1)}, u32[]{:S(2)}) copy-start(f32[1,1024]{1,0:T(1,128)S(1)} %get-tuple-element.992) | copy-start | bytes 12292
  276.3 70.2 %all-gather.19.cloned.1.call-start = ((), (), s32[]{:S(2)}) async-start(), calls=%async_computation.19 | async-start | bytes 3063808 | tf_op jit(solution)/shard_map/all_gather | solution.py:296
  277.1 114.7 %all-gather.21.cloned.1.call-start = ((), (), s32[]{:S(2)}) async-start(), calls=%async_computation.20 | async-start | bytes 3063808 | tf_op jit(solution)/shard_map/all_gather | solution.py:297
  277.9 159.2 %all-gather.23.cloned.1.call-start = ((), (), s32[]{:S(2)}) async-start(), calls=%async_computation.21 | async-start | bytes 3063808 | tf_op jit(solution)/shard_map/all_gather | solution.py:298
  278.6 180.9 %reduce-scatter.22.cloned.1.call-start = ((), (), s32[]{:S(2)}) async-start(), calls=%async_computation.23 | async-start | bytes 786432 | tf_op jit(solution)/shard_map/reduce_scatter | solution.py:322
  302.4 159.0 %copy-start.129 = (f32[128]{0:T(128)}, f32[128]{0:T(128)S(1)}, u32[]{:S(2)}) copy-start(f32[128]{0:T(128)S(1)} %add_rsqrt_fusion.2) | copy-start | bytes 1540
  446.4 323.8 %reduce-scatter.24.cloned.1.call-start = ((), (), s32[]{:S(2)}) async-start(), calls=%async_computation.24 | async-start | bytes 786432 | tf_op jit(solution)/shard_map/reduce_scatter | solution.py:359
  755.5 74.4 %reduce-scatter.40.cloned.1.call-start = ((), (), s32[]{:S(2)}) async-start(), calls=%async_computation.32 | async-start | bytes 557056
  756.8 88.9 %reduce-scatter.20.cloned.1.call-start = ((), (), s32[]{:S(2)}) async-start(), calls=%async_computation.22 | async-start | bytes 786432 | tf_op jit(solution)/shard_map/reduce_scatter | solution.py:306
  760.6 215.8 %all-reduce.39.cloned.1.call-start = ((), (), s32[]{:S(2)}) async-start(), calls=%async_computation.34 | async-start | bytes 151552 | tf_op jit(solution)/shard_map/psum | solution.py:382
  772.1 272.2 %reduce-scatter.28.cloned.1.call-start = ((), (), s32[]{:S(2)}) async-start(), calls=%async_computation.26 | async-start | bytes 2228224 | tf_op jit(solution)/shard_map/reduce_scatter | solution.py:367
  774.0 335.5 %reduce-scatter.26.cloned.1.call-start = ((), (), s32[]{:S(2)}) async-start(), calls=%async_computation.25 | async-start | bytes 2228224 | tf_op jit(solution)/shard_map/reduce_scatter | solution.py:366
  775.8 409.4 %reduce-scatter.34.cloned.1.call-start = ((), (), s32[]{:S(2)}) async-start(), calls=%async_computation.29 | async-start | bytes 4456448 | tf_op jit(solution)/shard_map/reduce_scatter | solution.py:371
  778.7 482.8 %reduce-scatter.30.cloned.1.call-start = ((), (), s32[]{:S(2)}) async-start(), calls=%async_computation.27 | async-start | bytes 4456448 | tf_op jit(solution)/shard_map/reduce_scatter | solution.py:368
  782.5 554.9 %reduce-scatter.32.cloned.1.call-start = ((), (), s32[]{:S(2)}) async-start(), calls=%async_computation.28 | async-start | bytes 4456448 | tf_op jit(solution)/shard_map/reduce_scatter | solution.py:369
  785.3 637.6 %reduce-scatter.36.cloned.1.call-start = ((), (), s32[]{:S(2)}) async-start(), calls=%async_computation.30 | async-start | bytes 6127616 | tf_op jit(solution)/shard_map/reduce_scatter | solution.py:185
  790.1 718.5 %reduce-scatter.38.cloned.1.call-start = ((), (), s32[]{:S(2)}) async-start(), calls=%async_computation.31 | async-start | bytes 6127616 | tf_op jit(solution)/shard_map/reduce_scatter | solution.py:186
  794.7 799.7 %reduce-scatter.42.cloned.1.call-start = ((), (), s32[]{:S(2)}) async-start(), calls=%async_computation.33 | async-start | bytes 6127616
  (222 other events, 2735.2 us)
Sparse Core Ops, SparseCore 0:
  10.3 41.0 all-gather.12
  53.5 37.2 all-gather.8
  93.0 40.3 all-gather.10
  135.3 40.4 all-gather.14
  177.9 40.7 all-gather.16
  276.5 24.6 reduce-scatter.17
  303.7 42.7 all-gather.18
  349.0 42.6 all-gather.20
  394.3 42.6 all-gather.22
  446.5 12.8 reduce-scatter.21
  755.6 14.5 reduce-scatter.23
  774.0 55.8 reduce-scatter.39
  832.1 13.5 reduce-scatter.19
  854.3 122.0 all-reduce.38
  980.6 63.6 reduce-scatter.27
  1048.9 60.5 reduce-scatter.25
  1113.8 71.3 reduce-scatter.33
  1190.0 71.5 reduce-scatter.29
  1266.0 71.3 reduce-scatter.31
  1342.2 80.6 reduce-scatter.35
  1427.9 80.7 reduce-scatter.37
  1513.6 80.7 reduce-scatter.41
where the time goes:
time: 1620 us; the launch traced here: 1610 us
  waiting for transfers between devices  1010 us (62%)
  other arithmetic  246 us (15%)
  matrix products  185 us (11%)
  local copies, waits for them, and re-layouts  81.6 us (5%)
  blocking collectives  67.9 us (4%)
  between operations  16.2 us (1%)
    another operation x32, other arithmetic, segment_update(): lax.linalg.triangular_solve(system, target, left_side=True, lower=True, t...  167 us
    psum x1, waiting for transfers between devices, per_device(): lax.psum((grad_gain_in, place_part(grad_conv_q, conv_query, 1), place_par...  129 us
    unnamed x24, waiting for transfers between devices  115 us
    reduce_scatter x1, waiting for transfers between devices, sum_ffn_grads(): lax.psum_scatter(grad_fup_w, 'dp', scatter_dimension=0, tiled=True)  85.7 us
    reduce_scatter x1, waiting for transfers between devices, sum_ffn_grads(): lax.psum_scatter(grad_fgate_w, 'dp', scatter_dimension=0, tiled=True)  85.5 us
    reduce_scatter x1, waiting for transfers between devices, per_device(): lax.psum_scatter(grad_w_value, 'dp', scatter_dimension=0, tiled=True)  76.4 us
    reduce_scatter x1, waiting for transfers between devices, per_device(): lax.psum_scatter(grad_w_gate, 'dp', scatter_dimension=0, tiled=True)  75.8 us
    reduce_scatter x1, waiting for transfers between devices, per_device(): lax.psum_scatter(grad_out_turned, 'dp', scatter_dimension=0, tiled=True)  75.7 us
  transfers between devices with their start and end apart: 22, of which 20 were waited for; matrix products, arithmetic and copies ran while one was open for 12% of the time, Pallas kernels for 0%

commit v1 on v0

v1 whole, which is shorter than its diff:
```python
import functools

import jax
import jax.numpy as jnp
from jax import lax
from jax.experimental import pallas as pl
from jax.experimental.pallas import tpu as pltpu
from jax.sharding import PartitionSpec as P

norm_epsilon = 1e-06
LANES = 128
BASE = 8
f32 = jnp.float32
bf16 = jnp.bfloat16
NN = ((1,), (0,))
NT = ((1,), (1,))
TN = ((0,), (0,))


def rms_rows(matrix):
    return matrix * lax.rsqrt(jnp.mean(matrix * matrix, axis=-1, keepdims=True) + norm_epsilon)


def rms_back(matrix, incoming, gain):
    scale = lax.rsqrt(jnp.mean(matrix * matrix, axis=-1, keepdims=True) + norm_epsilon)
    normed = matrix * scale
    scaled = incoming * gain
    grad_matrix = scale * (scaled - normed * jnp.mean(scaled * normed, axis=-1, keepdims=True))
    return (grad_matrix, jnp.sum(incoming * normed, axis=0))


def dot(left, right, dims):
    return lax.dot_general(left, right, (dims, ((), ())), preferred_element_type=f32)


def contract_last(left, right):
    return dot(left, right, NT)


def contract_first(left, right):
    return dot(left, right, TN)


def split(value):
    high = value.astype(bf16)
    return (high, (value - high.astype(f32)).astype(bf16))


def mul(left, right, dims=NN):
    return dot(left[0], right[0], dims) + (
        dot(left[0], right[1], dims) + dot(left[1], right[0], dims)
    )


def mask_mul(mask, value, dims, mask_first=True):
    first = value.astype(bf16)
    rest = value - first.astype(f32)
    second = rest.astype(bf16)
    third = (rest - second.astype(f32)).astype(bf16)
    total = None
    for part in (third, second, first):
        term = dot(mask, part, dims) if mask_first else dot(part, mask, dims)
        total = term if total is None else total + term
    return total


def silu_back(value, sig):
    return sig * (1.0 + value * (1.0 - sig))


def tap_masks(ids_col):
    length = ids_col.shape[0]
    row = lax.broadcasted_iota(jnp.int32, (length, 1), 0)
    masks = [None]
    for offset in range(1, 4):
        shifted = pltpu.roll(jnp.broadcast_to(ids_col, (length, LANES)), offset, 0)[:, :1]
        masks.append(jnp.logical_and(row >= offset, shifted == ids_col).astype(f32))
    return masks


def conv_pre(signal, taps, masks):
    total = signal * taps[3:4]
    for offset in range(1, 4):
        total = total + pltpu.roll(signal, offset, 0) * taps[3 - offset : 4 - offset] * masks[offset]
    return total


def conv_back(signal, taps, masks, grad):
    length = signal.shape[0]
    grad_signal = grad * taps[3:4]
    rows = [jnp.sum(grad * signal, axis=0, keepdims=True)]
    for offset in range(1, 4):
        masked = grad * masks[offset]
        rows.append(jnp.sum(masked * pltpu.roll(signal, offset, 0), axis=0, keepdims=True))
        grad_signal = (
            grad_signal + pltpu.roll(masked, length - offset, 0) * taps[3 - offset : 4 - offset]
        )
    return (grad_signal, rows)


def unit(conv, factor):
    scale = lax.rsqrt(jnp.sum(conv * conv, axis=-1, keepdims=True) + norm_epsilon)
    return (conv * (scale * factor), scale)


def unit_back(conv, scale, factor, grad):
    inner = jnp.sum(grad * conv, axis=-1, keepdims=True) * scale * scale
    return (scale * factor) * (grad - conv * inner)


def pair_masks(ids_col, ids_row):
    length = ids_col.shape[0]
    row = lax.broadcasted_iota(jnp.int32, (length, length), 0)
    col = lax.broadcasted_iota(jnp.int32, (length, length), 1)
    same = ids_col == ids_row
    lower = jnp.logical_and(row >= col, same).astype(f32)
    strict = jnp.logical_and(row > col, same).astype(f32)
    return (row, col, lower, strict)


def decay_parts(block, a_row, dt_row, heads):
    lane = lax.broadcasted_iota(jnp.int32, block.shape, 1)
    shifted = block + dt_row
    soft = jnp.maximum(shifted, 0.0) + jnp.log1p(jnp.exp(-jnp.abs(shifted)))
    logs = jnp.where(lane < heads, -jnp.exp(a_row) * soft, 0.0)
    return (lane, shifted, logs)


def unit_lower_inverses(systems, row, col):
    length = row.shape[0]
    eye = (row == col).astype(f32)
    near = ((row // BASE) == (col // BASE)).astype(f32)
    blocks = [system * near for system in systems]
    parts = [split(block) for block in blocks]
    squares = [split(mul(part, part)) for part in parts]
    fourths = [split(mul(square, square)) for square in squares]
    inverses = [eye - block for block in blocks]
    inverses = [inv + mul(split(inv), square) for inv, square in zip(inverses, squares)]
    inverses = [inv + mul(split(inv), fourth) for inv, fourth in zip(inverses, fourths)]
    size = BASE
    while size < length:
        off = jnp.logical_and(
            (row // (2 * size)) == (col // (2 * size)), (row // size) != (col // size)
        ).astype(f32)
        held = [split(inv) for inv in inverses]
        steps = [split(mul(split(system * off), part)) for system, part in zip(systems, held)]
        inverses = [inv - mul(part, step) for inv, part, step in zip(inverses, held, steps)]
        size *= 2
    return inverses


def core_common(dims, proj, ids_col, ids_row, taps_q, taps_k, taps_v, a_row, dt_row):
    heads, key_dim, value_dim = dims
    keys, values = (heads * key_dim, heads * value_dim)
    masks = tap_masks(ids_col)
    row, col, lower, strict = pair_masks(ids_col, ids_row)
    tail = proj[:, 2 * keys + 2 * values :]
    lane, shifted, logs = decay_parts(tail, a_row, dt_row, heads)
    gates = jax.nn.sigmoid(tail)
    low_mask = lower.astype(bf16)
    cum = mask_mul(low_mask, logs, NN)
    cum_turned = mask_mul(low_mask, logs, ((0,), (1,)), mask_first=False)
    pre_q = conv_pre(proj[:, :keys], taps_q, masks)
    pre_k = conv_pre(proj[:, keys : 2 * keys], taps_k, masks)
    pre_v = conv_pre(proj[:, 2 * keys : 2 * keys + values], taps_v, masks)
    per_head = []
    for head in range(heads):
        span = slice(head * key_dim, (head + 1) * key_dim)
        wide = slice(head * value_dim, (head + 1) * value_dim)
        pq, pk, pv = (pre_q[:, span], pre_k[:, span], pre_v[:, wide])
        sq, sk, sv = (jax.nn.sigmoid(pq), jax.nn.sigmoid(pk), jax.nn.sigmoid(pv))
        cq, ck, value = (pq * sq, pk * sk, pv * sv)
        query, scale_q = unit(cq, key_dim ** (-0.5))
        keyvec, scale_k = unit(ck, 1.0)
        query_s, key_s = (split(query), split(keyvec))
        strength = gates[:, heads + head : heads + head + 1]
        within = jnp.exp(
            jnp.minimum(cum[:, head : head + 1] - cum_turned[head : head + 1, :], 0.0)
        )
        per_head.append(
            dict(
                pq=pq, pk=pk, pv=pv, sq=sq, sk=sk, sv=sv, cq=cq, ck=ck, value=value,
                scale_q=scale_q, scale_k=scale_k, query_s=query_s, key_s=key_s,
                strength=strength, w_low=within * lower, w_strict=within * strict,
                kk=mul(key_s, key_s, NT), qk=mul(query_s, key_s, NT),
                gate=proj[:, 2 * keys + values + head * value_dim :][:, :value_dim],
            )
        )
    return (per_head, masks, row, col, lane, shifted, logs, gates, low_mask)


def core_forward(
    dims, proj, ids_col, ids_row, taps_q, taps_k, taps_v, a_row, dt_row, gain, gated, inverse
):
    heads, _, value_dim = dims
    per_head, _, row, col, *_ = core_common(
        dims, proj[...], ids_col[...], ids_row[...], taps_q[...], taps_k[...], taps_v[...],
        a_row[...], dt_row[...],
    )
    inverses = unit_lower_inverses(
        [item["strength"] * item["kk"] * item["w_strict"] for item in per_head], row, col
    )
    for head, item in enumerate(per_head):
        inverse[head] = inverses[head]
        solved = mul(split(inverses[head]), split(item["strength"] * item["value"]))
        mixed = mul(split(item["qk"] * item["w_low"]), split(solved))
        scale = lax.rsqrt(jnp.mean(mixed * mixed, axis=-1, keepdims=True) + norm_epsilon)
        gate = item["gate"]
        gated[:, head * value_dim : (head + 1) * value_dim] = (
            mixed * scale * gain[...] * (gate * jax.nn.sigmoid(gate))
        ).astype(bf16)


def core_backward(
    dims, proj, ids_col, ids_row, taps_q, taps_k, taps_v, a_row, dt_row, gain, inverse, grad_out,
    grad_proj, grad_q, grad_k, grad_v, grad_small,
):
    heads, key_dim, value_dim = dims
    keys, values = (heads * key_dim, heads * value_dim)
    raw = proj[...]
    tq, tk, tv, gains = (taps_q[...], taps_k[...], taps_v[...], gain[...])
    per_head, masks, row, col, lane, shifted, logs, gates, low_mask = core_common(
        dims, raw, ids_col[...], ids_row[...], tq, tk, tv, a_row[...], dt_row[...]
    )
    grad_cum = jnp.zeros(logs.shape, f32)
    grad_gates = jnp.zeros(logs.shape, f32)
    grad_gain = jnp.zeros(gains.shape, f32)
    for head, item in enumerate(per_head):
        span = slice(head * key_dim, (head + 1) * key_dim)
        wide = slice(head * value_dim, (head + 1) * value_dim)
        strength, value, gate = (item["strength"], item["value"], item["gate"])
        turned = split(inverse[head])
        solved = mul(turned, split(strength * value))
        solved_s = split(solved)
        attend = item["qk"] * item["w_low"]
        attend_s = split(attend)
        mixed = mul(attend_s, solved_s)
        scale = lax.rsqrt(jnp.mean(mixed * mixed, axis=-1, keepdims=True) + norm_epsilon)
        normed = mixed * scale
        sig = jax.nn.sigmoid(gate)
        incoming = grad_out[:, wide]
        through = incoming * (gate * sig)
        grad_gate = incoming * normed * gains * silu_back(gate, sig)
        grad_gain = grad_gain + jnp.sum(through * normed, axis=0, keepdims=True)
        scaled = through * gains
        grad_mixed = scale * (
            scaled - normed * jnp.mean(scaled * normed, axis=-1, keepdims=True)
        )
        grad_s = split(grad_mixed)
        grad_attend = mul(grad_s, solved_s, NT)
        grad_target = mul(turned, split(mul(attend_s, grad_s, TN)), TN)
        grad_system = -mul(split(grad_target), solved_s, NT) * item["w_strict"]
        weighted = grad_system * item["kk"]
        energy = grad_attend * attend + strength * weighted
        cum_grad = jnp.sum(energy - jnp.transpose(energy), axis=1, keepdims=True)
        strength_grad = jnp.sum(weighted, axis=1, keepdims=True) + jnp.sum(
            grad_target * value, axis=1, keepdims=True
        )
        grad_cum = jnp.where(lane == head, cum_grad, grad_cum)
        grad_gates = jnp.where(lane == heads + head, strength_grad, grad_gates)
        grad_qk = split(grad_attend * item["w_low"])
        grad_kk = grad_system * strength
        grad_kk = split(grad_kk + jnp.transpose(grad_kk))
        query_grad = mul(grad_qk, item["key_s"])
        key_grad = mul(grad_qk, item["query_s"], TN) + mul(grad_kk, item["key_s"])
        back_q = unit_back(item["cq"], item["scale_q"], key_dim ** (-0.5), query_grad)
        back_k = unit_back(item["ck"], item["scale_k"], 1.0, key_grad)
        back_q = back_q * silu_back(item["pq"], item["sq"])
        back_k = back_k * silu_back(item["pk"], item["sk"])
        back_v = strength * grad_target * silu_back(item["pv"], item["sv"])
        for start, width, taps, where, back, out in (
            (0, span, tq, head * key_dim, back_q, grad_q),
            (keys, span, tk, head * key_dim, back_k, grad_k),
            (2 * keys, wide, tv, head * value_dim, back_v, grad_v),
        ):
            size = back.shape[1]
            signal = raw[:, start + where : start + where + size]
            low_grad, tap_rows = conv_back(signal, taps[:, width], masks, back)
            grad_proj[:, start + where : start + where + size] = low_grad.astype(bf16)
            for offset in range(4):
                out[3 - offset : 4 - offset, width] = tap_rows[offset]
        place = 2 * keys + values + head * value_dim
        grad_proj[:, place : place + value_dim] = grad_gate.astype(bf16)
    grad_logs = mask_mul(low_mask, grad_cum, TN)
    grad_shift = grad_logs * -jnp.exp(a_row[...]) * jax.nn.sigmoid(shifted)
    grad_shift = jnp.where(lane < heads, grad_shift, 0.0)
    tail = grad_shift + grad_gates * gates * (1.0 - gates)
    grad_proj[:, 2 * keys + 2 * values :] = tail.astype(bf16)
    grad_small[...] = jnp.zeros(grad_small.shape, f32)
    grad_small[0:1, :] = grad_gain
    grad_small[1:2, :LANES] = jnp.sum(grad_logs * logs, axis=0, keepdims=True)
    grad_small[2:3, :LANES] = jnp.sum(grad_shift, axis=0, keepdims=True)


def core_params():
    return pltpu.CompilerParams(vmem_limit_bytes=56 * 1024 * 1024)


def call_forward(dims, length, operands):
    heads, _, value_dim = dims
    return pl.pallas_call(
        functools.partial(core_forward, dims),
        out_shape=(
            jax.ShapeDtypeStruct((length, heads * value_dim), bf16),
            jax.ShapeDtypeStruct((heads, length, length), f32),
        ),
        compiler_params=core_params(),
        cost_estimate=pl.CostEstimate(
            flops=120 * heads * length**3, bytes_accessed=6 * 1024 * 1024, transcendentals=1000000
        ),
        name="core_forward",
    )(*operands)


def call_backward(dims, length, operands):
    heads, key_dim, value_dim = dims
    keys, values = (heads * key_dim, heads * value_dim)
    return pl.pallas_call(
        functools.partial(core_backward, dims),
        out_shape=(
            jax.ShapeDtypeStruct((length, 2 * keys + 2 * values + LANES), bf16),
            jax.ShapeDtypeStruct((4, keys), f32),
            jax.ShapeDtypeStruct((4, keys), f32),
            jax.ShapeDtypeStruct((4, values), f32),
            jax.ShapeDtypeStruct((8, value_dim), f32),
        ),
        compiler_params=core_params(),
        cost_estimate=pl.CostEstimate(
            flops=120 * heads * length**3, bytes_accessed=8 * 1024 * 1024, transcendentals=1000000
        ),
        name="core_backward",
    )(*operands)


def swap(value):
    return lax.ppermute(value, "tensor", [(0, 1), (1, 0)])


def both_halves(own, rank):
    other = swap(own)
    first = jnp.where(rank == 0, own, other)
    second = jnp.where(rank == 0, other, own)
    return jnp.concatenate([first, second], axis=0)


def sum_halves(terms, rank):
    rows = terms.shape[0] // 2
    sent = lax.dynamic_slice_in_dim(terms, (1 - rank) * rows, rows, 0).astype(bf16)
    kept = lax.dynamic_slice_in_dim(terms, rank * rows, rows, 0)
    return kept + swap(sent).astype(f32)


def sum_everywhere(value, groups):
    value = value + swap(value)
    step = 1
    while step < groups:
        value = value + lax.ppermute(value, "dp", [(i, i ^ step) for i in range(groups)])
        step *= 2
    return value


def per_device(
    groups,
    inputs,
    segment_ids,
    gain_in,
    w_query,
    w_key,
    w_value,
    w_gate,
    w_decay,
    conv_query,
    conv_key,
    conv_value,
    a_log,
    dt_bias,
    gain_mix,
    w_out,
    gain_ffn,
    w_ffn_gate,
    w_ffn_up,
    w_ffn_down,
    out_grad,
):
    rank = lax.axis_index("tensor")
    heads = w_decay.shape[2]
    keys = w_query.shape[1]
    values = w_value.shape[1]
    hidden_units = w_ffn_gate.shape[1]
    rows_held = w_query.shape[0]
    dims = (heads, keys // heads, values // heads)
    length = segment_ids.shape[0]

    mixer_held = jnp.concatenate(
        [
            w_query, w_key, w_value, w_gate, w_decay.reshape(rows_held, 2 * heads),
            jnp.zeros((rows_held, LANES - 2 * heads), bf16),
        ],
        axis=1,
    )
    full_mixer = lax.all_gather(mixer_held, "dp", axis=0, tiled=True)
    block_held = jnp.concatenate([w_out.T, w_ffn_gate, w_ffn_up, w_ffn_down.T], axis=1)
    full_block = lax.all_gather(block_held, "dp", axis=0, tiled=True)
    out_turned = full_block[:, :values]
    full_pair = full_block[:, values : values + 2 * hidden_units]
    down_turned = full_block[:, values + 2 * hidden_units :]

    inputs_wide = inputs.astype(f32)
    normed_in = both_halves((rms_rows(inputs_wide) * gain_in).astype(bf16), rank)
    grad_rows_out = both_halves(out_grad, rank)

    def part(whole, width, along):
        return lax.dynamic_slice_in_dim(whole, rank * width, width, along)

    def lane_row(vector):
        return jnp.pad(part(vector, heads, 0), (0, LANES - heads)).reshape(1, LANES)

    proj = jnp.dot(normed_in, full_mixer, preferred_element_type=f32)
    operands = (
        proj, segment_ids.reshape(length, 1), segment_ids.reshape(1, length),
        part(conv_query, keys, 1), part(conv_key, keys, 1), part(conv_value, values, 1),
        lane_row(a_log), lane_row(dt_bias), gain_mix.reshape(1, -1),
    )
    mixed_gated, inverse = call_forward(dims, length, operands)
    residual = inputs_wide + sum_halves(contract_last(mixed_gated, out_turned), rank)
    normed_mid = both_halves((rms_rows(residual) * gain_ffn).astype(bf16), rank)
    ffn_pair = jnp.dot(normed_mid, full_pair, preferred_element_type=f32)
    ffn_gate, ffn_up = (ffn_pair[:, :hidden_units], ffn_pair[:, hidden_units:])
    sigmoid_gate = jax.nn.sigmoid(ffn_gate)
    hidden = (ffn_gate * sigmoid_gate * ffn_up).astype(bf16)
    output = (residual + sum_halves(contract_last(hidden, down_turned), rank)).astype(bf16)
    grad_hidden = jnp.dot(grad_rows_out, down_turned, preferred_element_type=f32)
    grad_pair = jnp.concatenate(
        [
            (grad_hidden * ffn_up * silu_back(ffn_gate, sigmoid_gate)).astype(bf16),
            (grad_hidden * (ffn_gate * sigmoid_gate)).astype(bf16),
        ],
        axis=1,
    )
    grad_mid = sum_halves(contract_last(grad_pair, full_pair), rank)
    grad_mid_rows, grad_gain_ffn = rms_back(residual, grad_mid, gain_ffn)
    grad_resid = out_grad.astype(f32) + grad_mid_rows
    grad_rows_mid = both_halves(grad_resid.astype(bf16), rank)
    block_grads = jnp.concatenate(
        [
            contract_first(grad_rows_mid, mixed_gated).astype(bf16),
            contract_first(normed_mid, grad_pair).astype(bf16),
            contract_first(grad_rows_out, hidden).astype(bf16),
        ],
        axis=1,
    )
    block_shard = lax.psum_scatter(block_grads, "dp", scatter_dimension=0, tiled=True).astype(f32)
    grad_mixed = jnp.dot(grad_rows_mid, out_turned, preferred_element_type=f32)
    grad_proj, grad_conv_q, grad_conv_k, grad_conv_v, grad_small = call_backward(
        dims, length, operands + (inverse, grad_mixed)
    )
    mixer_grads = contract_first(normed_in, grad_proj).astype(bf16)
    mixer_shard = lax.psum_scatter(mixer_grads, "dp", scatter_dimension=0, tiled=True).astype(f32)
    grad_in = sum_halves(contract_last(grad_proj, full_mixer), rank)
    grad_in_rows, grad_gain_in = rms_back(inputs_wide, grad_in, gain_in)
    grad_inputs = grad_resid + grad_in_rows

    def place_part(part_grad, whole):
        along = whole.ndim - 1
        return lax.dynamic_update_slice_in_dim(
            jnp.zeros(whole.shape, f32), part_grad, rank * part_grad.shape[along], along
        )

    small_parts = (
        grad_gain_in,
        place_part(grad_conv_q, conv_query),
        place_part(grad_conv_k, conv_key),
        place_part(grad_conv_v, conv_value),
        place_part(grad_small[1, :heads], a_log),
        place_part(grad_small[2, :heads], dt_bias),
        grad_small[0],
        grad_gain_ffn,
    )
    flat = jnp.concatenate([item.reshape(-1) for item in small_parts])
    padding = -flat.shape[0] % (8 * LANES)
    flat = sum_everywhere(jnp.pad(flat, (0, padding)).reshape(-1, LANES), groups).reshape(-1)
    small, at = ([], 0)
    for item in small_parts:
        small.append(flat[at : at + item.size].reshape(item.shape))
        at += item.size
    at_up, at_down = (values + hidden_units, values + 2 * hidden_units)
    at_decay = 2 * keys + 2 * values
    return (
        output,
        grad_inputs,
        small[0],
        mixer_shard[:, :keys],
        mixer_shard[:, keys : 2 * keys],
        mixer_shard[:, 2 * keys : 2 * keys + values],
        mixer_shard[:, 2 * keys + values : at_decay],
        mixer_shard[:, at_decay : at_decay + 2 * heads].reshape(rows_held, 2, heads),
        small[1],
        small[2],
        small[3],
        small[4],
        small[5],
        small[6],
        block_shard[:, :values].T,
        small[7],
        block_shard[:, values:at_up],
        block_shard[:, at_up:at_down],
        block_shard[:, at_down:].T,
    )


def solution(mesh):
    placed = (
        P(("dp", "tensor"), None),
        P("dp"),
        P(),
        P("dp", "tensor"),
        P("dp", "tensor"),
        P("dp", "tensor"),
        P("dp", "tensor"),
        P("dp", None, "tensor"),
        P(),
        P(),
        P(),
        P(),
        P(),
        P(),
        P("tensor", "dp"),
        P(),
        P("dp", "tensor"),
        P("dp", "tensor"),
        P("tensor", "dp"),
        P(("dp", "tensor"), None),
    )
    return jax.shard_map(
        functools.partial(per_device, mesh.shape["dp"]),
        mesh=mesh,
        in_specs=placed,
        out_specs=(
            P(("dp", "tensor"), None),
            P(("dp", "tensor"), None),
            P(),
            P("dp", "tensor"),
            P("dp", "tensor"),
            P("dp", "tensor"),
            P("dp", "tensor"),
            P("dp", None, "tensor"),
            P(),
            P(),
            P(),
            P(),
            P(),
            P(),
            P("tensor", "dp"),
            P(),
            P("dp", "tensor"),
            P("dp", "tensor"),
            P("tensor", "dp"),
        ),
        check_vma=False,
    )
```

time: 1620 us -> 479 us (0.30)
  waiting for transfers between devices: 1010 us -> 327 us
  other arithmetic: 246 us -> 16.4 us
  matrix products: 185 us -> 37.7 us
  blocking collectives: 67.9 us -> 0 us
  local copies, waits for them, and re-layouts: 81.6 us -> 27.6 us
  Pallas kernels: 0 us -> 28.9 us
  starting transfers between devices: 1.1 us -> 17.4 us
    reduce_scatter x11 -> x2, waiting for transfers between devices: 573 us -> 141 us  [the longest x1 120 us: per_device(): lax.psum_scatter(block_grads, 'dp', scatter_dimension=0, tiled=True)]
    another operation x53 -> x0, other arithmetic: 184 us -> none  [the longest x32 167 us: segment_update(): lax.linalg.triangular_solve(system, target, left_side=True, lower=True, t...]
    psum x1 -> x0, waiting for transfers between devices: 129 us -> none  [per_device(): lax.psum((grad_gain_in, place_part(grad_conv_q, conv_query, 1), place_par...]
    dot_general x119 -> x12, matrix products: 159 us -> 37.7 us  [the longest x8 23.7 us: dot(): lax.dot_general(left, right, (dims, ((), ())), preferred_element_type=f32)]
    unnamed x24 -> x4, waiting for transfers between devices: 115 us -> 0.07 us
    all_gather x5 -> x0, blocking collectives: 67.9 us -> none  [the longest x1 23.8 us: per_device(): lax.all_gather(w_decay, 'dp', axis=0, tiled=True)]
    all_gather x8 -> x2, waiting for transfers between devices: 192 us -> 126 us  [the longest x1 71.2 us: per_device(): full_block = lax.all_gather(block_held, 'dp', axis=0, tiled=True)]
    ppermute x0 -> x13, waiting for transfers between devices: none -> 59.4 us  [the longest x9 39.8 us: swap(): return lax.ppermute(value, 'tensor', [(0, 1), (1, 0)])]
  transfers between devices with their start and end apart: 22 -> 17, of which waited for: 20 -> 17; matrix products, arithmetic and copies ran while one was open for 12% -> 11% of each run, Pallas kernels for 0% -> 3%
where the time goes in v1:
time: 479 us; the launch traced here: 470 us
  waiting for transfers between devices  327 us (68%)
  matrix products  37.7 us (8%)
  Pallas kernels  28.9 us (6%)
  local copies, waits for them, and re-layouts  27.6 us (6%)
  starting transfers between devices  17.4 us (4%)
  other arithmetic  16.4 us (3%)
  between operations  14.7 us (3%)
    reduce_scatter x1, waiting for transfers between devices, per_device(): lax.psum_scatter(block_grads, 'dp', scatter_dimension=0, tiled=True)  120 us
    all_gather x1, waiting for transfers between devices, per_device(): full_block = lax.all_gather(block_held, 'dp', axis=0, tiled=True)  71.2 us
    all_gather x1, waiting for transfers between devices, per_device(): full_mixer = lax.all_gather(mixer_held, 'dp', axis=0, tiled=True)  55 us
    ppermute x9, waiting for transfers between devices, swap(): return lax.ppermute(value, 'tensor', [(0, 1), (1, 0)])  39.8 us
    dot_general x8, matrix products, dot(): lax.dot_general(left, right, (dims, ((), ())), preferred_element_type=f32)  23.7 us
    reduce_scatter x1, waiting for transfers between devices, per_device(): lax.psum_scatter(mixer_grads, 'dp', scatter_dimension=0, tiled=True)  21.7 us
    ppermute x4, waiting for transfers between devices, sum_everywhere(): lax.ppermute(value, 'dp', [(i, i ^ step) for i in range(groups)])  19.7 us
    pallas_call x1, Pallas kernels, call_backward(): pl.pallas_call(functools.partial(core_backward, dims), out_shape=(jax.Sha...  16.2 us
  transfers between devices with their start and end apart: 17, of which 17 were waited for; matrix products, arithmetic and copies ran while one was open for 11% of the time, Pallas kernels for 3%

profile of v1, /device:TPU:0, one launch (start us, length us, event | category | flops | bytes accessed | tf_op | source)
XLA Modules:
  0.0 469.7 jit_solution(17987772276604550391)
XLA Ops:
  12.5 3.0 collective-permute-start
  18.3 3.6 collective-permute-done
  22.1 55.0 %all-gather.3.cloned.1.call-done = bf16[1024,3200]{1,0:T(8,128)(2,1)} async-done(((bf16[64,3200]{1,0:T(8,128)(2,1)}), bf16[1024,3200]{1,0:T(8,128)(2,1)}) %all-gather.3.cloned.1.call-update) | async-done | bytes 6553616 | tf_op jit(solution)/shard_map/all_gather | solution.py:401
  77.1 6.4 %fusion.24.proj = f32[256,3200]{1,0:T(8,128)} fusion(bf16[1024,3200]{1,0:T(8,128)(2,1)} %all-gather.3.cloned.1.call-done, bf16[128,1024]{1,0:T(8,128)(2,1)S(1)} %get-tuple-element.73, bf16[128,1024]{1,0:T(8,128)(2,1)S(1)} %get-tuple-element.72), kind=kOutput, calls=%fused_computation.55 | convolution fusion | flops 1678770176 | bytes 10354688 | tf_op jit(solution)/shard_map/dot_general | solution.py:418
  83.5 12.7 %core_forward.1 = (bf16[256,1024]{1,0:T(8,128)(2,1)}, f32[4,256,256]{2,1,0:T(8,128)}) custom-call(f32[256,3200]{1,0:T(8,128)} %fusion.24.proj, s32[256,1]{1,0:T(8,128)} %copy.43.ids_col, s32[1,256]{1,0:T(1,128)} %bitcast.61, f32[4,512]{1,0:T(4,128)} %get-tuple-element.83.taps_q, f32[4,512]{1,0:T(4,128)} %get-tuple-element.82.taps_k, ...), custom_call_target="tpu_custom_call" | custom-call | flops 8053063680 | bytes 6291456 | tf_op jit(solution)/shard_map/core_forward/pallas_call | solution.py:301
  96.3 71.2 %all-gather.5.cloned.1.call-done = bf16[1024,5248]{1,0:T(8,128)(2,1)} async-done(((bf16[64,5248]{1,0:T(8,128)(2,1)}), bf16[1024,5248]{1,0:T(8,128)(2,1)}) %all-gather.5.cloned.1.call-update) | async-done | bytes 10747920 | tf_op jit(solution)/shard_map/all_gather | solution.py:403
  172.3 7.1 %collective-permute-done.1 = bf16[128,1024]{1,0:T(8,128)(2,1)S(1)} collective-permute-done((bf16[128,1024]{1,0:T(8,128)(2,1)S(1)}, bf16[128,1024]{1,0:T(8,128)(2,1)S(1)}, u32[]{:S(2)}, u32[]{:S(2)}) %collective-permute-start.1) | collective-permute-done | bytes 262176 | tf_op jit(solution)/shard_map/ppermute | solution.py:336
  181.3 3.8 collective-permute-done.4
  185.1 4.9 %collective-permute-done.2 = bf16[128,1024]{1,0:T(8,128)(2,1)S(1)} collective-permute-done((bf16[128,1024]{1,0:T(8,128)(2,1)S(1)}, bf16[128,1024]{1,0:T(8,128)(2,1)S(1)}, u32[]{:S(2)}, u32[]{:S(2)}) %collective-permute-start.2) | collective-permute-done | bytes 262176 | tf_op jit(solution)/shard_map/ppermute | solution.py:336
  190.2 4.4 fusion.2
  202.3 6.1 %collective-permute-done.5 = bf16[128,1024]{1,0:T(8,128)(2,1)S(1)} collective-permute-done((bf16[128,1024]{1,0:T(8,128)(2,1)S(1)}, bf16[128,1024]{1,0:T(8,128)(2,1)S(1)}, u32[]{:S(2)}, u32[]{:S(2)}) %collective-permute-start.5) | collective-permute-done | bytes 262176 | tf_op jit(solution)/shard_map/ppermute | solution.py:336
  208.7 3.8 collective-permute-done.3
  215.1 5.2 %collective-permute-done.6 = bf16[128,1024]{1,0:T(8,128)(2,1)S(1)} collective-permute-done((bf16[128,1024]{1,0:T(8,128)(2,1)S(1)}, bf16[128,1024]{1,0:T(8,128)(2,1)S(1)}, u32[]{:S(2)}, u32[]{:S(2)}) %collective-permute-start.6) | collective-permute-done | bytes 262176 | tf_op jit(solution)/shard_map/ppermute | solution.py:336
  222.1 16.2 %core_backward.1 = (bf16[256,3200]{1,0:T(8,128)(2,1)}, f32[4,512]{1,0:T(4,128)}, f32[4,512]{1,0:T(4,128)}, f32[4,1024]{1,0:T(4,128)}, f32[8,256]{1,0:T(8,128)}) custom-call(f32[256,3200]{1,0:T(8,128)} %fusion.24.proj, s32[256,1]{1,0:T(8,128)} %copy.43.ids_col, s32[1,256]{1,0:T(1,128)} %bitcast.62, f32[4,512]{1,0:T(4,128)} %get-tuple-element.83.taps_q, ...), custom_call_target="tpu_custom_call" | custom-call | flops 8053063680 | bytes 8388608 | tf_op jit(solution)/shard_map/core_backward/pallas_call | solution.py:318
  238.4 6.1 %convolution_convert_fusion = bf16[1024,3200]{1,0:T(8,128)(2,1)} fusion(bf16[256,3200]{1,0:T(8,128)(2,1)} %get-tuple-element.28, bf16[128,1024]{1,0:T(8,128)(2,1)S(1)} %get-tuple-element.73, bf16[128,1024]{1,0:T(8,128)(2,1)S(1)} %get-tuple-element.72), kind=kOutput, calls=%fused_computation.1 | convolution fusion | flops 1682046976 | bytes 8716288 | tf_op jit(solution)/shard_map/dot_general | solution.py:33
  245.8 4.3 convolution_convert_fusion.1
  253.5 4.1 copy.46
  257.6 9.1 %pad_maximum_fusion = bf16[1024,5248]{1,0:T(8,128)(2,1)} fusion(bf16[1024,1408]{1,0:T(8,128)(2,1)S(1)} %convolution_convert_fusion.2, bf16[1024,2816]{1,0:T(8,128)(2,1)} %convolution_convert_fusion.1, bf16[1024,1024]{1,0:T(8,128)(2,1)} %copy.46), kind=kLoop, calls=%fused_computation | loop fusion | flops 32243712 | bytes 21495808 | tf_op jit(solution)/shard_map/concatenate | solution.py:444
  268.2 4.8 %fusion.41 = f32[256,1024]{1,0:T(8,128)S(1)} fusion(bf16[256,3200]{1,0:T(8,128)(2,1)S(1)} %copy-done.5, bf16[1024,3200]{1,0:T(8,128)(2,1)} %all-gather.3.cloned.1.call-done), kind=kOutput, calls=%fused_computation.99 | convolution fusion | flops 1677721600 | bytes 9240576 | tf_op jit(solution)/shard_map/dot_general | solution.py:33
  286.3 6.0 %collective-permute-done.10 = f32[152,128]{1,0:T(8,128)S(1)} collective-permute-done((f32[152,128]{1,0:T(8,128)S(1)}, f32[152,128]{1,0:T(8,128)S(1)}, u32[]{:S(2)}, u32[]{:S(2)}) %collective-permute-start.10) | collective-permute-done | bytes 77856 | tf_op jit(solution)/shard_map/ppermute | solution.py:357
  293.2 3.7 collective-permute-done.11
  299.9 8.7 %collective-permute-done.12 = f32[152,128]{1,0:T(8,128)S(1)} collective-permute-done((f32[152,128]{1,0:T(8,128)S(1)}, f32[152,128]{1,0:T(8,128)S(1)}, u32[]{:S(2)}, u32[]{:S(2)}) %collective-permute-start.12) | collective-permute-done | bytes 77856 | tf_op jit(solution)/shard_map/ppermute | solution.py:357
  313.0 21.7 %reduce-scatter.3.cloned.1.call-done = bf16[64,3200]{1,0:T(8,128)(2,1)} async-done(((bf16[1024,3200]{1,0:T(8,128)(2,1)}), bf16[64,3200]{1,0:T(8,128)(2,1)}) %reduce-scatter.3.cloned.1.call-update) | async-done | bytes 409616 | tf_op jit(solution)/shard_map/reduce_scatter | solution.py:458
  339.5 119.6 %reduce-scatter.5.cloned.1.call-done = bf16[64,5248]{1,0:T(8,128)(2,1)} async-done(((bf16[1024,5248]{1,0:T(8,128)(2,1)}), bf16[64,5248]{1,0:T(8,128)(2,1)}) %reduce-scatter.5.cloned.1.call-update) | async-done | bytes 671760 | tf_op jit(solution)/shard_map/reduce_scatter | solution.py:452
  (160 shorter events, 63.4 us)
Async XLA Ops:
  7.3 10.4 %copy-start.25 = (f32[4,1024]{1,0:T(4,128)S(1)}, f32[4,1024]{1,0:T(4,128)}, u32[]{:S(2)}) copy-start(f32[4,1024]{1,0:T(4,128)} %param.29) | copy-start | bytes 49156
  7.3 69.8 %all-gather.3.cloned.1.call-start = ((), (), s32[]{:S(2)}) async-start(), calls=%async_computation.2 | async-start | bytes 6963200 | tf_op jit(solution)/shard_map/all_gather | solution.py:401
  10.0 157.4 %all-gather.5.cloned.1.call-start = ((), (), s32[]{:S(2)}) async-start(), calls=%async_computation.3 | async-start | bytes 11419648 | tf_op jit(solution)/shard_map/all_gather | solution.py:403
  12.2 322.5 %reduce-scatter.3.cloned.1.call-start = ((), (), s32[]{:S(2)}) async-start(), calls=%async_computation.4 | async-start | bytes 6963200 | tf_op jit(solution)/shard_map/reduce_scatter | solution.py:458
  12.5 9.3 %collective-permute-start = (bf16[128,1024]{1,0:T(8,128)(2,1)S(1)}, bf16[128,1024]{1,0:T(8,128)(2,1)S(1)}, u32[]{:S(2)}, u32[]{:S(2)}) collective-permute-start(bf16[128,1024]{1,0:T(8,128)(2,1)S(1)} %fusion.17), channel_id=1, source_target_pairs={{0,1},{1,0},{2,3},{3,2},{4,5},{5,4},{6,7},{7,6},{8,9},{9,8},{10,11... | collective-permute-start | bytes 786440 | tf_op jit(solution)/shard_map/ppermute | solution.py:336
  96.3 75.5 %copy-start.12 = (bf16[128,1024]{1,0:T(8,128)(2,1)S(1)}, bf16[128,1024]{1,0:T(8,128)(2,1)}, u32[]{:S(2)}) copy-start(bf16[128,1024]{1,0:T(8,128)(2,1)} %param.39) | copy-start | bytes 786436
  167.5 12.2 %copy-start.20 = (f32[1024]{0:T(1024)S(1)}, f32[1024]{0:T(1024)}, u32[]{:S(2)}) copy-start(f32[1024]{0:T(1024)} %param.35) | copy-start | bytes 12292
  170.2 9.2 %collective-permute-start.1 = (bf16[128,1024]{1,0:T(8,128)(2,1)S(1)}, bf16[128,1024]{1,0:T(8,128)(2,1)S(1)}, u32[]{:S(2)}, u32[]{:S(2)}) collective-permute-start(bf16[128,1024]{1,0:T(8,128)(2,1)S(1)} %dynamic-slice_convert_fusion.3), channel_id=1, source_target_pairs={{0,1},{1,0},{2,3},{3,2},{4,5},{5,4},{6,7},{7,6},{8,9},{9,8},{10,11... | collective-permute-start | bytes 786440 | tf_op jit(solution)/shard_map/ppermute | solution.py:336
  171.8 13.3 %collective-permute-start.4 = (bf16[128,1024]{1,0:T(8,128)(2,1)S(1)}, bf16[128,1024]{1,0:T(8,128)(2,1)S(1)}, u32[]{:S(2)}, u32[]{:S(2)}) collective-permute-start(bf16[128,1024]{1,0:T(8,128)(2,1)S(1)} %copy-done.12), channel_id=1, source_target_pairs={{0,1},{1,0},{2,3},{3,2},{4,5},{5,4},{6,7},{7,6},{8,9},{9,8},{10,11... | collective-permute-start | bytes 786440 | tf_op jit(solution)/shard_map/ppermute | solution.py:336
  179.7 10.2 %collective-permute-start.2 = (bf16[128,1024]{1,0:T(8,128)(2,1)S(1)}, bf16[128,1024]{1,0:T(8,128)(2,1)S(1)}, u32[]{:S(2)}, u32[]{:S(2)}) collective-permute-start(bf16[128,1024]{1,0:T(8,128)(2,1)S(1)} %multiply_convert_fusion.3), channel_id=1, source_target_pairs={{0,1},{1,0},{2,3},{3,2},{4,5},{5,4},{6,7},{7,6},{8,9},{9,8},{10,11... | collective-permute-start | bytes 786440 | tf_op jit(solution)/shard_map/ppermute | solution.py:336
  199.1 9.3 %collective-permute-start.5 = (bf16[128,1024]{1,0:T(8,128)(2,1)S(1)}, bf16[128,1024]{1,0:T(8,128)(2,1)S(1)}, u32[]{:S(2)}, u32[]{:S(2)}) collective-permute-start(bf16[128,1024]{1,0:T(8,128)(2,1)S(1)} %dynamic-slice_convert_fusion.1), channel_id=1, source_target_pairs={{0,1},{1,0},{2,3},{3,2},{4,5},{5,4},{6,7},{7,6},{8,9},{9,8},{10,11... | collective-permute-start | bytes 786440 | tf_op jit(solution)/shard_map/ppermute | solution.py:336
  201.7 10.7 %collective-permute-start.3 = (bf16[128,1024]{1,0:T(8,128)(2,1)S(1)}, bf16[128,1024]{1,0:T(8,128)(2,1)S(1)}, u32[]{:S(2)}, u32[]{:S(2)}) collective-permute-start(bf16[128,1024]{1,0:T(8,128)(2,1)S(1)} %dynamic-slice_convert_fusion.2), channel_id=1, source_target_pairs={{0,1},{1,0},{2,3},{3,2},{4,5},{5,4},{6,7},{7,6},{8,9},{9,8},{10,11... | collective-permute-start | bytes 786440 | tf_op jit(solution)/shard_map/ppermute | solution.py:336
  213.6 6.7 %collective-permute-start.6 = (bf16[128,1024]{1,0:T(8,128)(2,1)S(1)}, bf16[128,1024]{1,0:T(8,128)(2,1)S(1)}, u32[]{:S(2)}, u32[]{:S(2)}) collective-permute-start(bf16[128,1024]{1,0:T(8,128)(2,1)S(1)} %get-tuple-element.56), channel_id=1, source_target_pairs={{0,1},{1,0},{2,3},{3,2},{4,5},{5,4},{6,7},{7,6},{8,9},{9,8},{10,11... | collective-permute-start | bytes 786440 | tf_op jit(solution)/shard_map/ppermute | solution.py:336
  220.4 17.9 %copy-start.8 = (bf16[128,1024]{1,0:T(8,128)(2,1)}, bf16[128,1024]{1,0:T(8,128)(2,1)S(1)}, u32[]{:S(2)}) copy-start(bf16[128,1024]{1,0:T(8,128)(2,1)S(1)} %get-tuple-element.65) | copy-start | bytes 786436
  220.4 17.9 %copy-start.10 = (bf16[128,1024]{1,0:T(8,128)(2,1)}, bf16[128,1024]{1,0:T(8,128)(2,1)S(1)}, u32[]{:S(2)}) copy-start(bf16[128,1024]{1,0:T(8,128)(2,1)S(1)} %get-tuple-element.66) | copy-start | bytes 786436
  244.5 214.6 %reduce-scatter.5.cloned.1.call-start = ((), (), s32[]{:S(2)}) async-start(), calls=%async_computation.5 | async-start | bytes 11419648 | tf_op jit(solution)/shard_map/reduce_scatter | solution.py:452
  273.0 25.9 %copy-start.4 = (f32[128,1024]{1,0:T(8,128)S(1)}, f32[128,1024]{1,0:T(8,128)}, u32[]{:S(2)}) copy-start(f32[128,1024]{1,0:T(8,128)} %get-tuple-element.57) | copy-start | bytes 1572868
  273.1 6.4 %collective-permute-start.7 = (bf16[128,1024]{1,0:T(8,128)(2,1)S(1)}, bf16[128,1024]{1,0:T(8,128)(2,1)S(1)}, u32[]{:S(2)}, u32[]{:S(2)}) collective-permute-start(bf16[128,1024]{1,0:T(8,128)(2,1)S(1)} %dynamic-slice_convert_fusion), channel_id=1, source_target_pairs={{0,1},{1,0},{2,3},{3,2},{4,5},{5,4},{6,7},{7,6},{8,9},{9,8},{10,11... | collective-permute-start | bytes 786440 | tf_op jit(solution)/shard_map/ppermute | solution.py:336
  279.9 4.5 collective-permute-start.8
  284.4 1.3 collective-permute-start.9
  285.7 6.7 %collective-permute-start.10 = (f32[152,128]{1,0:T(8,128)S(1)}, f32[152,128]{1,0:T(8,128)S(1)}, u32[]{:S(2)}, u32[]{:S(2)}) collective-permute-start(f32[152,128]{1,0:T(8,128)S(1)} %fusion.50), channel_id=1, source_target_pairs={{0,4},{2,6},{4,0},{6,2},{8,12},{10,14},{12,8},{14,10},{16,20},{18,... | collective-permute-start | bytes 233480 | tf_op jit(solution)/shard_map/ppermute | solution.py:357
  292.4 4.5 collective-permute-start.11
  296.9 11.8 %collective-permute-start.12 = (f32[152,128]{1,0:T(8,128)S(1)}, f32[152,128]{1,0:T(8,128)S(1)}, u32[]{:S(2)}, u32[]{:S(2)}) collective-permute-start(f32[152,128]{1,0:T(8,128)S(1)} %add.121), channel_id=1, source_target_pairs={{0,16},{2,18},{4,20},{6,22},{8,24},{10,26},{12,28},{14,30},{16,0},... | collective-permute-start | bytes 233480 | tf_op jit(solution)/shard_map/ppermute | solution.py:357
  336.0 126.7 %copy-start.1 = (f32[4,2048]{1,0:T(4,128)S(1)}, f32[4,2048]{1,0:T(4,128)}, u32[]{:S(2)}) copy-start(f32[4,2048]{1,0:T(4,128)} %param.30) | copy-start | bytes 98308
  (24 other events, 117.2 us)
Sparse Core Ops, SparseCore 0:
  11.0 66.0 all-gather.2
  79.4 88.0 all-gather.4
  244.6 89.9 reduce-scatter.2
  339.1 119.9 reduce-scatter.4
